TPU v7x, 128 devices: a whole 4x4x4 slice. The times are simulated.
128 devices in a mesh: row: 16 (over y, x), col: 8 (over z, core).
Axes of the slice: x: 4, y: 4, z: 4, core: 2. Of those that a mesh axis runs over, the one named last changes fastest.
Arguments:
- panel: float32 [64, 65536], P(None, ('row', 'col')), may hold values from -6 to 6
- blocks: bfloat16 [256, 8, 8, 256, 256], P('row', 'col'), may hold values from -100 to 100
- columns: int32 [256, 8, 8], P('row', 'col'), may hold values from 0 to 31
- counts: int32 [256, 8], P('row', 'col'), may hold values from 1 to 8, as said below
Outputs:
- basis: float32 [64, 65536], P(None, ('row', 'col'))
Inputs may be any that keep to these rules, and one draw needn't show every extreme that they name: `counts`: every block row has between 1 and 8 live slots in each column group, and both ends occur.
All inputs are finite; a program needn't handle non-finite values.
Results may differ from a plain program's by a relative error of at most 0.008.
Values may be sent and summed in bfloat16 or wider, within the bound.
A program may use at most 64 MiB of HBM per device.

v0:
```python
import jax
import jax.numpy as jnp
from jax import lax
from jax.sharding import PartitionSpec as P

STEPS = 2


def per_device(panel, blocks, columns, counts):
    stored = blocks[:, 0]
    slot_cols = columns[:, 0]
    row_blocks, slot_count, block_size = (stored.shape[0], stored.shape[1], stored.shape[2])
    vectors = panel.shape[0]
    alive = (jnp.arange(slot_count, dtype=jnp.int32)[None, :] < counts).astype(jnp.bfloat16)
    partial_degree = jnp.einsum(
        "bkrs,bk->br", jnp.abs(stored), alive, preferred_element_type=jnp.float32
    ).reshape(-1)
    degree = lax.psum_scatter(partial_degree, "col", scatter_dimension=0, tiled=True)
    scale = 1.0 / jnp.sqrt(degree)
    own_width = panel.shape[1]
    total_sites = own_width * lax.axis_size("row") * lax.axis_size("col")
    state = panel
    for step in range(STEPS):
        sent = (scale[None, :] * state).astype(jnp.bfloat16)
        whole = lax.all_gather(sent, "row", axis=1, tiled=True)
        grid = whole.reshape(vectors, -1, block_size)
        picked = grid[:, slot_cols.reshape(-1), :].reshape(
            vectors, row_blocks, slot_count, block_size
        )
        picked = picked * alive[None, :, :, None]
        prod = jnp.einsum("pbks,bkrs->pbr", picked, stored, preferred_element_type=jnp.float32)
        prod = prod.reshape(vectors, row_blocks * block_size)
        mine = lax.psum_scatter(prod, "col", scatter_dimension=1, tiled=True)
        grown = scale[None, :] * mine
        gram_local = jnp.dot(grown, grown.T, precision=lax.Precision.HIGHEST)
        gram = lax.psum(gram_local, ("row", "col")) / total_sites
        lower = jnp.linalg.cholesky(gram)
        state = lax.linalg.triangular_solve(lower, grown, left_side=True, lower=True)
    return state


def solution(mesh):
    in_specs = (
        P(None, ("row", "col")),
        P("row", "col", None, None, None),
        P("row", "col", None),
        P("row", "col"),
    )
    out_specs = P(None, ("row", "col"))
    return jax.shard_map(
        per_device, mesh=mesh, in_specs=in_specs, out_specs=out_specs, check_vma=False
    )
```

profile of v0, /device:TPU:1, one launch (start us, length us, event | category | flops | bytes accessed | tf_op | source)
XLA Modules:
  0.0 388.8 jit_solution(7181804151273590126)
XLA Ops:
  7.3 7.7 %convert_reduce_fusion = bf16[16,8,256]{2,1,0:T(8,128)(2,1)S(1)} fusion(bf16[16,1,8,256,256]{4,3,2,1,0:T(8,128)(2,1)} %param.8), kind=kLoop, calls=%fused_computation.2 | loop fusion | flops 33521664 | bytes 16842752 | tf_op jit(solution)/shard_map/bkrs,bk->br/reduce_sum | solution.py:15
  15.1 24.9 %all-reduce = f32[4096]{0:T(1024)S(1)} all-reduce(f32[4096]{0:T(1024)S(1)} %bitcast.81), channel_id=2, replica_groups=mesh['row'=16,'col'=8] {'col'}, use_global_device_ids=true, to_apply=%region_1.0.clone | all-reduce | flops 4096 | bytes 32768
  42.2 43.5 %all-gather.3.cloned.1.call-done = bf16[64,8192]{1,0:T(8,128)(2,1)} async-done(((bf16[64,512]{1,0:T(8,128)(2,1)}), bf16[64,8192]{1,0:T(8,128)(2,1)}) %all-gather.3.cloned.1.call-update) | async-done | bytes 1048592 | tf_op jit(solution)/shard_map/all_gather | solution.py:25
  85.7 1.3 copy.48
  87.1 2.7 gather_fusion
  89.8 10.8 %fusion.8 = f32[16,8,8,256]{3,2,1,0:T(8,128)S(1)} fusion(bf16[16,1,8,256,256]{4,3,2,1,0:T(8,128)(2,1)} %param.8, bf16[64,16,8,256]{3,0,2,1:T(8,128)(2,1)} %bitcast.75, bf16[16,8]{1,0:T(8,128)(2,1)S(1)} %get-tuple-element.6), kind=kOutput, calls=%fused_computation.12 | convolution fusion | flops 1075838976 | bytes 22020352 | tf_op jit(solution)/shard_map/pbks,bkrs->pbr/dot_general | solution.py:31
  100.6 1.1 copy.39
  101.7 30.0 %reduce-scatter.3.cloned.1.call-done = f32[64,512]{1,0:T(8,128)} async-done(((f32[64,4096]{1,0:T(8,128)}), f32[64,512]{1,0:T(8,128)}) %reduce-scatter.3.cloned.1.call-update) | async-done | bytes 131088 | tf_op jit(solution)/shard_map/reduce_scatter | solution.py:33
  131.8 1.2 fusion.24
  133.0 67.5 %psum.14 = f32[64,64]{0,1:T(8,128)S(1)} all-reduce(f32[64,64]{0,1:T(8,128)S(1)} %fusion.24), channel_id=1, replica_groups=mesh['row'=16,'col'=8] {'row','col'}, use_global_device_ids=true, to_apply=%region_3.0 | all-reduce | flops 4096 | bytes 32768 | tf_op jit(solution)/shard_map/psum | solution.py:36
  200.7 5.8 %cholesky.44 = f32[64,64]{1,0:T(8,128)S(1)} custom-call(f32[64,64]{1,0:T(8,128)S(1)} %fusion.35), custom_call_target="Cholesky" | custom-call | tf_op jit(solution)/shard_map/jit(cholesky)/cholesky | solution.py:37
  207.9 4.9 %custom-call.6 = f32[1,64,64]{1,2,0:T(8,128)S(1)} custom-call(f32[1,64,64]{2,1,0:T(8,128)S(1)} %fusion.30), custom_call_target="InvertDiagBlocksLowerTriangular" | custom-call | tf_op jit(solution)/shard_map/triangular_solve/custom-call.0 | solution.py:38
  212.8 1.9 fusion.18
  214.7 38.4 %all-gather.5.cloned.1.call-done = bf16[64,8192]{1,0:T(8,128)(2,1)} async-done(((bf16[64,512]{1,0:T(8,128)(2,1)}), bf16[64,8192]{1,0:T(8,128)(2,1)}) %all-gather.5.cloned.1.call-update) | async-done | bytes 1048592 | tf_op jit(solution)/shard_map/all_gather | solution.py:25
  253.1 1.3 copy.47
  254.4 2.7 gather_fusion.1
  257.2 10.8 %fusion.13 = f32[16,8,8,256]{3,2,1,0:T(8,128)S(1)} fusion(bf16[16,1,8,256,256]{4,3,2,1,0:T(8,128)(2,1)} %param.8, bf16[64,16,8,256]{3,0,2,1:T(8,128)(2,1)} %bitcast.74, bf16[16,8]{1,0:T(8,128)(2,1)S(1)} %get-tuple-element.6), kind=kOutput, calls=%fused_computation.13 | convolution fusion | flops 1075838976 | bytes 22020352 | tf_op jit(solution)/shard_map/pbks,bkrs->pbr/dot_general | solution.py:31
  267.9 1.1 copy.40
  269.1 30.1 %reduce-scatter.5.cloned.1.call-done = f32[64,512]{1,0:T(8,128)} async-done(((f32[64,4096]{1,0:T(8,128)}), f32[64,512]{1,0:T(8,128)}) %reduce-scatter.5.cloned.1.call-update) | async-done | bytes 131088 | tf_op jit(solution)/shard_map/reduce_scatter | solution.py:33
  299.1 1.2 fusion.21
  300.4 67.8 %psum.15 = f32[64,64]{0,1:T(8,128)S(1)} all-reduce(f32[64,64]{0,1:T(8,128)S(1)} %fusion.21), channel_id=1, replica_groups=mesh['row'=16,'col'=8] {'row','col'}, use_global_device_ids=true, to_apply=%region_7.10 | all-reduce | flops 4096 | bytes 32768 | tf_op jit(solution)/shard_map/psum | solution.py:36
  368.3 5.8 %cholesky.55 = f32[64,64]{1,0:T(8,128)S(1)} custom-call(f32[64,64]{1,0:T(8,128)S(1)} %fusion.33), custom_call_target="Cholesky" | custom-call | tf_op jit(solution)/shard_map/jit(cholesky)/cholesky | solution.py:37
  375.5 4.9 %custom-call.7 = f32[1,64,64]{1,2,0:T(8,128)S(1)} custom-call(f32[1,64,64]{2,1,0:T(8,128)S(1)} %fusion.31), custom_call_target="InvertDiagBlocksLowerTriangular" | custom-call | tf_op jit(solution)/shard_map/triangular_solve/custom-call.0 | solution.py:38
  380.4 1.9 fusion.19
  (37 shorter events, 5.4 us)
Async XLA Ops:
  6.5 79.2 %all-gather.3.cloned.1.call-start = ((), (), s32[]{:S(2)}) async-start(), calls=%async_computation.2 | async-start | bytes 1114112 | tf_op jit(solution)/shard_map/all_gather | solution.py:25
  7.3 32.7 %copy-start.2 = (u32[128]{0:T(128)S(1)}, u32[128]{0:T(128)}, u32[]{:S(2)}) copy-start(u32[128]{0:T(128)} %constant.45) | copy-start | bytes 1540
  7.3 34.0 %copy-start = (f32[64,512]{1,0:T(8,128)S(1)}, f32[64,512]{1,0:T(8,128)}, u32[]{:S(2)}) copy-start(f32[64,512]{1,0:T(8,128)} %param.7) | copy-start | bytes 393220
  7.3 34.7 %copy-start.1 = (s32[16,1,8]{0,2,1:T(8,128)S(1)}, s32[16,1,8]{0,2,1:T(8,128)}, u32[]{:S(2)}) copy-start(s32[16,1,8]{0,2,1:T(8,128)} %param.9) | copy-start | bytes 1540
  42.0 89.8 %reduce-scatter.3.cloned.1.call-start = ((), (), s32[]{:S(2)}) async-start(), calls=%async_computation.3 | async-start | bytes 1179648 | tf_op jit(solution)/shard_map/reduce_scatter | solution.py:33
  101.7 151.4 %all-gather.5.cloned.1.call-start = ((), (), s32[]{:S(2)}) async-start(), calls=%async_computation.4 | async-start | bytes 1114112 | tf_op jit(solution)/shard_map/all_gather | solution.py:25
  214.7 84.5 %reduce-scatter.5.cloned.1.call-start = ((), (), s32[]{:S(2)}) async-start(), calls=%async_computation.5 | async-start | bytes 1179648 | tf_op jit(solution)/shard_map/reduce_scatter | solution.py:33
Sparse Core Ops, SparseCore 0:
  42.1 43.5 all-gather.2
  101.8 29.9 reduce-scatter.2
  214.8 38.2 all-gather.4
  269.2 29.9 reduce-scatter.4
where the time goes:
time: 389 us
  blocking collectives  160 us (41%)
  waiting for transfers between devices  142 us (37%)
  other arithmetic  33.2 us (9%)
  matrix products  27.9 us (7%)
  between operations  13.9 us (4%)
  local copies, waits for them, and re-layouts  11.3 us (3%)
    psum x2, blocking collectives, per_device(): gram = lax.psum(gram_local, ('row', 'col')) / total_sites  135 us
    all_gather x2, waiting for transfers between devices, per_device(): whole = lax.all_gather(sent, 'row', axis=1, tiled=True)  81.9 us
    reduce_scatter x2, waiting for transfers between devices, per_device(): mine = lax.psum_scatter(prod, 'col', scatter_dimension=1, tiled=True)  60.1 us
    unnamed x1, blocking collectives  24.9 us
    dot_general x2, matrix products, per_device(): jnp.einsum('pbks,bkrs->pbr', picked, stored, preferred_element_type=jnp.f...  21.5 us
    another operation x6, other arithmetic, per_device(): lower = jnp.linalg.cholesky(gram)  13 us
    another operation x4, other arithmetic, per_device(): lax.linalg.triangular_solve(lower, grown, left_side=True, lower=True)  11.1 us
  transfers between devices with their start and end apart: 4, of which 4 were waited for; matrix products, arithmetic and copies ran while one was open for 0% of the time, Pallas kernels for 0%

commit v1 on v0

v1 whole, which is shorter than its diff:
```python
import functools

import jax
import jax.numpy as jnp
from jax import lax
from jax.experimental import pallas as pl
from jax.experimental.pallas import tpu as pltpu
from jax.sharding import PartitionSpec as P

MESH = pl.DeviceIdType.MESH
HIGHEST = lax.Precision.HIGHEST
F32 = jnp.float32
BF16 = jnp.bfloat16
NT = (((1,), (1,)), ((), ()))
TN = (((0,), (0,)), ((), ()))
SIDE = 4
PANEL = 16

COL_ORDER = ((2, 0), (2, 1), (1, 0), (1, 1), (3, 0), (3, 1), (0, 1))
NEAR_FAR = (1, 3, 2)


def inverse_factor(gram):
    size = gram.shape[0]
    rows = lax.broadcasted_iota(jnp.int32, (size, size), 0)
    lanes = lax.broadcasted_iota(jnp.int32, (size, size), 1)
    whole = jnp.concatenate([gram, (rows == lanes).astype(F32)], axis=1)
    parts = [whole[t * PANEL : (t + 1) * PANEL] for t in range(size // PANEL)]
    below = lax.broadcasted_iota(jnp.int32, (PANEL, 2 * size), 0)
    done = []
    for t in range(len(parts)):
        part = parts[t]
        first = t * PANEL
        column = [jnp.broadcast_to(part[:, first + q : first + q + 1], part.shape) for q in range(PANEL)]
        pivot = jnp.zeros_like(part)
        for q in range(PANEL):
            pivot_row = column[q][q : q + 1]
            pivot = jnp.where(below == q, pivot_row, pivot)
            factor = jnp.where(below > q, column[q] / pivot_row, 0.0)
            part = part - factor * part[q : q + 1]
            for later in range(q + 1, PANEL):
                column[later] = column[later] - factor * column[later][q : q + 1]
        scaled = part / pivot
        for u in range(t + 1, len(parts)):
            parts[u] = parts[u] - lax.dot_general(
                scaled[:, u * PANEL : (u + 1) * PANEL], part, TN, precision=HIGHEST, preferred_element_type=F32
            )
        done.append(part[:, size:] * lax.rsqrt(pivot[:, size:]))
    return jnp.concatenate(done, axis=0)


def pack(gram):
    half = gram.shape[0] // 2
    return jnp.concatenate([gram[:half], gram[half:]], axis=1)


def unpack(packed):
    width = packed.shape[1] // 2
    return jnp.concatenate([packed[:, :width], packed[:, width:]], axis=0)


def kernel(
    panel, blocks, columns, counts, gram_out, grown_out,
    stored, first, second, scales, own_scale, deg_out, deg_in, part_out, part_in, part_own,
    gram_a_out, gram_a_in, gram_b_out, gram_b_in, grown,
    load_sem, deg_s, deg_r, scale_s, scale_r, gather_s, gather_r, part_s, part_r, ga_s, ga_r, gb_s, gb_r,
):
    row, col = lax.axis_index("row"), lax.axis_index("col")
    y, x = row // SIDE, row % SIDE
    z, core = col // 2, col % 2
    block_rows, slots = columns.shape[0], columns.shape[2]
    sites = 65536

    def chip(dy, dx):
        return ((y + dy) % SIDE) * SIDE + (x + dx) % SIDE

    def column_of(dz, dc):
        return ((z + dz) % SIDE) * 2 + (core + dc) % 2

    def source_of(dz, dc):
        return ((z + SIDE - dz) % SIDE) * 2 + (core + dc) % 2

    def send(src, dst, send_sem, recv_sem, to):
        return pltpu.make_async_remote_copy(
            src_ref=src, dst_ref=dst, send_sem=send_sem, recv_sem=recv_sem, device_id=to, device_id_type=MESH
        )

    loads = [
        pltpu.make_async_copy(blocks.at[i, 0], stored.at[pl.ds(i * slots, slots)], load_sem.at[i])
        for i in range(block_rows)
    ]
    for load in loads:
        load.start()

    barrier = pltpu.get_barrier_semaphore()
    row_offsets = [(dy, dx) for dy in (0, 1, 3, 2) for dx in (0, 1, 3, 2) if (dy, dx) != (0, 0)]
    for dy, dx in row_offsets:
        pl.semaphore_signal(barrier, inc=1, device_id=(chip(dy, dx), col), device_id_type=MESH)
    for dz, dc in COL_ORDER:
        pl.semaphore_signal(barrier, inc=1, device_id=(row, column_of(dz, dc)), device_id_type=MESH)

    mine = pl.ds(row * 2, 2)
    for half in range(2):
        first[row * 2 + half] = panel[:, half * 256 : (half + 1) * 256].astype(BF16)
    first[32] = jnp.zeros_like(first[32])
    second[32] = jnp.zeros_like(second[32])
    pl.semaphore_wait(barrier, len(row_offsets) + len(COL_ORDER))

    def forward(buf, turn, half, src, to, k):
        (sy, sx), (ty, tx) = src, to
        piece = chip(SIDE - sy, SIDE - sx) * 2 + half
        arrives = half * 16 + ((sy + ty) % SIDE) * SIDE + (sx + tx) % SIDE
        return send(buf.at[piece], buf.at[piece], gather_s.at[turn, k], gather_r.at[turn, arrives], (chip(ty, tx), col))

    def gather_start(buf, turn):
        copies = []
        for d in NEAR_FAR:
            copies.append(forward(buf, turn, 0, (0, 0), (0, d), len(copies)))
            copies[-1].start()
            copies.append(forward(buf, turn, 1, (0, 0), (d, 0), len(copies)))
            copies[-1].start()
        for d in NEAR_FAR:
            copies.append(forward(buf, turn, 0, (0, 0), (d, 0), len(copies)))
            copies[-1].start()
            copies.append(forward(buf, turn, 1, (0, 0), (0, d), len(copies)))
            copies[-1].start()
        return copies

    def arrived(buf, turn, half, dy, dx):
        piece = chip(SIDE - dy, SIDE - dx) * 2 + half
        send(
            buf.at[piece], buf.at[piece], gather_s.at[turn, 0], gather_r.at[turn, half * 16 + dy * SIDE + dx], (row, col)
        ).wait_recv()

    def gather_forward(buf, turn, copies):
        for d in NEAR_FAR:
            arrived(buf, turn, 0, 0, d)
            for e in NEAR_FAR:
                copies.append(forward(buf, turn, 0, (0, d), (e, 0), len(copies)))
                copies[-1].start()
            arrived(buf, turn, 1, d, 0)
            for e in NEAR_FAR:
                copies.append(forward(buf, turn, 1, (d, 0), (0, e), len(copies)))
                copies[-1].start()

    def gather_end(buf, turn, copies):
        for e in NEAR_FAR:
            for d in range(SIDE):
                arrived(buf, turn, 0, e, d)
                arrived(buf, turn, 1, d, e)
        for copy in copies:
            copy.wait_send()

    copies = gather_start(first, 0)

    for i in range(block_rows):
        loads[i].wait()
        total = jnp.zeros((8, 256), F32)
        for s in range(slots):
            alive = jnp.where(s < counts[i, 0], 1.0, 0.0).astype(F32)
            ones = jnp.full((8, 256), alive, F32).astype(BF16)
            total += lax.dot_general(ones, jnp.abs(stored[i * slots + s]), NT, preferred_element_type=F32)
        deg_out[i // 2, i % 2] = total[:1]
        if i == 11:
            gather_forward(first, 0, copies)

    deg_copies = []
    for k, (dz, dc) in enumerate(COL_ORDER):
        to = column_of(dz, dc)
        deg_copies.append(send(deg_out.at[to], deg_in.at[k], deg_s.at[k], deg_r.at[k], (row, to)))
        deg_copies[-1].start()
    degree = deg_out[col]
    for k, copy in enumerate(deg_copies):
        copy.wait_recv()
        degree = degree + deg_in[k]
    own_scale[...] = 1.0 / jnp.sqrt(degree)
    scales[mine] = own_scale[...]
    scale_copies = []
    for k, (dy, dx) in enumerate(row_offsets):
        scale_copies.append(
            send(own_scale, scales.at[mine], scale_s.at[k], scale_r.at[k], (chip(dy, dx), col))
        )
        scale_copies[-1].start()
    gather_end(first, 0, copies)
    for k, (dy, dx) in enumerate(row_offsets):
        theirs = pl.ds(chip(SIDE - dy, SIDE - dx) * 2, 2)
        send(own_scale, scales.at[theirs], scale_s.at[k], scale_r.at[k], (row, col)).wait_recv()

    def scale_block(g, carry):
        first[g] = (first[g].astype(F32) * scales[g]).astype(BF16)
        return carry

    lax.fori_loop(0, 32, scale_block, 0, unroll=4)

    def product(buf, turn):
        started = []
        for k, (dz, dc) in enumerate(COL_ORDER + ((0, 0),)):
            to = column_of(dz, dc)
            for half in range(2):
                i = to * 2 + half
                total = jnp.zeros((64, 256), F32)
                for s in range(slots):
                    g = jnp.where(s < counts[i, 0], columns[i, 0, s], 32)
                    total += lax.dot_general(buf[g], stored[i * slots + s], NT, preferred_element_type=F32)
                if k < len(COL_ORDER):
                    part_out[turn, k, half] = total.astype(BF16)
                else:
                    part_own[half] = total
            if k < len(COL_ORDER):
                started.append(
                    send(part_out.at[turn, k], part_in.at[turn, k], part_s.at[turn, k], part_r.at[turn, k], (row, to))
                )
                started[-1].start()
        return started

    def summed(started, turn):
        total = part_own[...]
        for k, copy in enumerate(started):
            copy.wait_recv()
            total = total + part_in[turn, k].astype(F32)
        for copy in started:
            copy.wait_send()
        return total

    def local_gram(values):
        return sum(
            lax.dot_general(values[h], values[h], NT, precision=HIGHEST, preferred_element_type=F32) for h in range(2)
        )

    def gram_col_start(gram, turn):
        gram_a_out[turn] = pack(gram)
        started = []
        for k, (dz, dc) in enumerate(COL_ORDER):
            started.append(
                send(
                    gram_a_out.at[turn], gram_a_in.at[turn, k], ga_s.at[turn, k], ga_r.at[turn, k],
                    (row, column_of(dz, dc)),
                )
            )
            started[-1].start()
        return started

    def gram_row_start(started, turn):
        total = gram_a_out[turn]
        for k, copy in enumerate(started):
            copy.wait_recv()
            total = total + gram_a_in[turn, k]
        gram_b_out[turn] = total
        onward = []
        for k, (dy, dx) in enumerate(row_offsets):
            onward.append(
                send(gram_b_out.at[turn], gram_b_in.at[turn, k], gb_s.at[turn, k], gb_r.at[turn, k], (chip(dy, dx), col))
            )
            onward[-1].start()
        for copy in started:
            copy.wait_send()
        return onward

    def gram_end(onward, turn):
        total = gram_b_out[turn]
        for k, copy in enumerate(onward):
            copy.wait_recv()
            total = total + gram_b_in[turn, k]
        for copy in onward:
            copy.wait_send()
        return unpack(total) / sites

    started = product(first, 0)
    for copy in deg_copies + scale_copies:
        copy.wait_send()
    grown[...] = summed(started, 0) * own_scale[...]
    second[mine] = (grown[...] * own_scale[...]).astype(BF16)
    copies = gather_start(second, 1)
    gram_copies = gram_col_start(local_gram(grown), 0)
    gather_forward(second, 1, copies)
    gram_copies = gram_row_start(gram_copies, 0)
    gather_end(second, 1, copies)

    started = product(second, 1)
    inverse = inverse_factor(gram_end(gram_copies, 0))
    raw = summed(started, 1) * own_scale[...]
    for half in range(2):
        grown[half] = jnp.dot(inverse, raw[half], precision=HIGHEST, preferred_element_type=F32)
    grown_out[...] = grown[...]
    gram_copies = gram_col_start(local_gram(grown), 1)
    gram_copies = gram_row_start(gram_copies, 1)
    gram_out[...] = gram_end(gram_copies, 1)


def finish(gram, grown, out):
    inverse = inverse_factor(gram[...])
    for half in range(2):
        out[:, half * 256 : (half + 1) * 256] = jnp.dot(
            inverse, grown[half], precision=HIGHEST, preferred_element_type=F32
        )


def per_device(panel, blocks, columns, counts):
    vmem = pl.BlockSpec(memory_space=pltpu.VMEM)
    smem = pl.BlockSpec(memory_space=pltpu.SMEM)
    dma = pltpu.SemaphoreType.DMA
    gram, grown = pl.pallas_call(
        kernel,
        out_shape=(jax.ShapeDtypeStruct((64, 64), F32), jax.ShapeDtypeStruct((2, 64, 256), F32)),
        in_specs=[vmem, pl.BlockSpec(memory_space=pl.ANY), smem, smem],
        out_specs=(vmem, vmem),
        scratch_shapes=[
            pltpu.VMEM((128, 256, 256), BF16),
            pltpu.VMEM((33, 64, 256), BF16),
            pltpu.VMEM((33, 64, 256), BF16),
            pltpu.VMEM((32, 1, 256), F32),
            pltpu.VMEM((2, 1, 256), F32),
            pltpu.VMEM((8, 2, 1, 256), F32),
            pltpu.VMEM((7, 2, 1, 256), F32),
            pltpu.VMEM((2, 7, 2, 64, 256), BF16),
            pltpu.VMEM((2, 7, 2, 64, 256), BF16),
            pltpu.VMEM((2, 64, 256), F32),
            pltpu.VMEM((2, 32, 128), F32),
            pltpu.VMEM((2, 7, 32, 128), F32),
            pltpu.VMEM((2, 32, 128), F32),
            pltpu.VMEM((2, 15, 32, 128), F32),
            pltpu.VMEM((2, 64, 256), F32),
            dma((16,)),
            dma((7,)),
            dma((7,)),
            dma((15,)),
            dma((15,)),
            dma((2, 30)),
            dma((2, 32)),
            dma((2, 7)),
            dma((2, 7)),
            dma((2, 7)),
            dma((2, 7)),
            dma((2, 15)),
            dma((2, 15)),
        ],
        compiler_params=pltpu.CompilerParams(
            collective_id=0, has_side_effects=True, vmem_limit_bytes=48 * 2**20
        ),
    )(panel, blocks, columns, counts)
    return pl.pallas_call(
        finish,
        out_shape=jax.ShapeDtypeStruct(panel.shape, F32),
        in_specs=[vmem, vmem],
        out_specs=vmem,
    )(gram, grown)


def solution(mesh):
    in_specs = (
        P(None, ("row", "col")),
        P("row", "col", None, None, None),
        P("row", "col", None),
        P("row", "col"),
    )
    return jax.shard_map(
        per_device, mesh=mesh, in_specs=in_specs, out_specs=P(None, ("row", "col")), check_vma=False
    )
```

time: 389 us -> 77.3 us (0.20)
  blocking collectives: 160 us -> 0 us
  waiting for transfers between devices: 142 us -> 0 us
  Pallas kernels: 0 us -> 73.5 us
  other arithmetic: 33.2 us -> 0 us
  matrix products: 27.9 us -> 0 us
  between operations: 13.9 us -> 0.02 us
  local copies, waits for them, and re-layouts: 11.3 us -> 3.63 us
    psum x2 -> x0, blocking collectives: 135 us -> none  [per_device(): gram = lax.psum(gram_local, ('row', 'col')) / total_sites]
    all_gather x2 -> x0, waiting for transfers between devices: 81.9 us -> none  [per_device(): whole = lax.all_gather(sent, 'row', axis=1, tiled=True)]
    pallas_call x0 -> x2, Pallas kernels: none -> 73.5 us  [the longest x1 69.6 us: per_device(): pl.pallas_call(kernel, out_shape=(jax.ShapeDtypeStruct((64, 64), F32), ja...]
    reduce_scatter x2 -> x0, waiting for transfers between devices: 60.1 us -> none  [per_device(): mine = lax.psum_scatter(prod, 'col', scatter_dimension=1, tiled=True)]
    unnamed x1 -> x0, blocking collectives: 24.9 us -> none
    dot_general x5 -> x0, matrix products: 24.2 us -> none  [the longest x2 21.5 us: per_device(): jnp.einsum('pbks,bkrs->pbr', picked, stored, preferred_element_type=jnp.f...]
    another operation x10 -> x0, other arithmetic: 24.1 us -> none  [the longest x6 13 us: per_device(): lower = jnp.linalg.cholesky(gram)]
    reduce_sum x1 -> x0, other arithmetic: 7.65 us -> none  [per_device(): jnp.einsum('bkrs,bk->br', jnp.abs(stored), alive, preferred_element_type=...]
  transfers between devices with their start and end apart: 4 -> 0, of which waited for: 4 -> 0; matrix products, arithmetic and copies ran while one was open for 0% -> 0% of each run, Pallas kernels for 0% -> 0%
where the time goes in v1:
time: 77.3 us; the launch traced here: 77.1 us
  Pallas kernels  73.5 us (95%)
  local copies, waits for them, and re-layouts  3.63 us (5%)
    pallas_call x1, Pallas kernels, per_device(): pl.pallas_call(kernel, out_shape=(jax.ShapeDtypeStruct((64, 64), F32), ja...  69.6 us
    pallas_call x1, Pallas kernels, per_device(): pl.pallas_call(finish, out_shape=jax.ShapeDtypeStruct(panel.shape, F32),...  3.92 us
    unnamed x8, local copies, waits for them, and re-layouts  3.63 us

profile of v1, /device:TPU:1, one launch (start us, length us, event | category | flops | bytes accessed | tf_op | source)
XLA Modules:
  0.0 77.1 jit_solution(1676145229127562420)
XLA Ops:
  0.0 0.8 copy.5.columns
  0.8 0.7 copy.6.counts
  1.5 0.0 copy-start
  1.5 0.9 %copy-done = f32[64,512]{1,0:T(8,128)S(1)} copy-done((f32[64,512]{1,0:T(8,128)S(1)}, f32[64,512]{1,0:T(8,128)}, u32[]{:S(2)}) %copy-start) | copy-done | bytes 131096
  2.4 69.6 %shard_map.46 = (f32[64,64]{1,0:T(8,128)S(1)}, f32[2,64,256]{2,1,0:T(8,128)S(1)}) custom-call(f32[64,512]{1,0:T(8,128)S(1)} %copy-done, bf16[16,1,8,256,256]{4,3,2,1,0:T(8,128)(2,1)} %blocks.1, s32[16,1,8]{2,1,0:T(1,128)S(1)} %copy.5.columns, s32[16,1]{1,0:T(8,128)S(1)} %copy.6.counts), custom_call_target="tpu_custom_call" | custom-call | tf_op jit(solution)/shard_map/pallas_call | solution.py:302
  72.0 0.0 copy-start.1
  72.0 0.6 copy-done.1
  72.6 0.0 copy-start.2
  72.6 0.6 copy-done.2
  73.2 3.9 %shard_map.47 = f32[64,512]{1,0:T(8,128)} custom-call(f32[64,64]{1,0:T(8,128)} %copy-done.2, f32[2,64,256]{2,1,0:T(8,128)} %copy-done.1), custom_call_target="tpu_custom_call" | custom-call | tf_op jit(solution)/shard_map/pallas_call | solution.py:341
Async XLA Ops:
  1.5 0.9 %copy-start = (f32[64,512]{1,0:T(8,128)S(1)}, f32[64,512]{1,0:T(8,128)}, u32[]{:S(2)}) copy-start(f32[64,512]{1,0:T(8,128)} %panel.1) | copy-start | bytes 393220
  72.0 0.6 copy-start.1
  72.6 0.6 copy-start.2

commit v2 on v0

v2 whole, which is shorter than its diff:
```python
import functools

import jax
import jax.numpy as jnp
from jax import lax
from jax.experimental import pallas as pl
from jax.experimental.pallas import tpu as pltpu
from jax.sharding import PartitionSpec as P

MESH = pl.DeviceIdType.MESH
HIGHEST = lax.Precision.HIGHEST
F32 = jnp.float32
BF16 = jnp.bfloat16
NT = (((1,), (1,)), ((), ()))
SIDE = 4
PANEL = 16

COL_ORDER = ((2, 0), (2, 1), (1, 0), (1, 1), (3, 0), (3, 1), (0, 1))
NEAR_FAR = (1, 3, 2)


def inverse_factor(gram):
    size = gram.shape[0]
    rows = lax.broadcasted_iota(jnp.int32, (size, size), 0)
    lanes = lax.broadcasted_iota(jnp.int32, (size, size), 1)
    rest = jnp.concatenate([gram, (rows == lanes).astype(F32)], axis=1)
    done = []
    for first in range(0, size, PANEL):
        below = lax.broadcasted_iota(jnp.int32, rest.shape, 0)
        column = [jnp.broadcast_to(rest[:, first + q : first + q + 1], rest.shape) for q in range(PANEL)]
        pivots = []
        for q in range(PANEL):
            pivot = column[q][q : q + 1]
            pivots.append(pivot)
            factor = jnp.where(below > q, column[q] * (1.0 / pivot), 0.0)
            rest = rest - factor * rest[q : q + 1]
            for later in range(q + 1, PANEL):
                column[later] = column[later] - factor * column[later][q : q + 1]
        done.append(rest[:PANEL, size:] * lax.rsqrt(jnp.concatenate(pivots, axis=0)[:, size:]))
        rest = rest[PANEL:]
    return jnp.concatenate(done, axis=0)


def pack(gram):
    half = gram.shape[0] // 2
    return jnp.concatenate([gram[:half], gram[half:]], axis=1)


def unpack(packed):
    width = packed.shape[1] // 2
    return jnp.concatenate([packed[:, :width], packed[:, width:]], axis=0)


def kernel(
    panel, blocks, columns_hbm, counts_hbm, out,
    stored, start, columns, counts, first, second, scales, own_scale, deg_out, deg_in, part_out, part_in, part_own,
    piece_out, piece_in, piece_sum, piece_row, piece_all, gram_out, gram_in, cross_out, cross_in, grown,
    small_sem, load_sem, deg_s, deg_r, scale_s, scale_r, gather_s, gather_r, part_s, part_r,
    pa_s, pa_r, pb_s, pb_r, pc_s, pc_r, ga_s, ga_r, gb_s, gb_r,
):
    row, col = lax.axis_index("row"), lax.axis_index("col")
    y, x = row // SIDE, row % SIDE
    z, core = col // 2, col % 2
    slots, block_rows = columns.shape
    sites = 65536

    def chip(dy, dx):
        return ((y + dy) % SIDE) * SIDE + (x + dx) % SIDE

    def column_of(dz, dc):
        return ((z + dz) % SIDE) * 2 + (core + dc) % 2

    def send(src, dst, send_sem, recv_sem, to):
        return pltpu.make_async_remote_copy(
            src_ref=src, dst_ref=dst, send_sem=send_sem, recv_sem=recv_sem, device_id=to, device_id_type=MESH
        )

    small = [
        pltpu.make_async_copy(panel, start, small_sem.at[0]),
        pltpu.make_async_copy(counts_hbm, counts, small_sem.at[1]),
        pltpu.make_async_copy(columns_hbm.at[0], columns, small_sem.at[2]),
    ]
    loads = [
        pltpu.make_async_copy(blocks.at[i, 0], stored.at[pl.ds(i * slots, slots)], load_sem.at[i])
        for i in range(block_rows)
    ]
    for load in small + loads:
        load.start()

    barrier = pltpu.get_barrier_semaphore()
    row_offsets = [(dy, dx) for dy in (2, 1, 3, 0) for dx in (2, 1, 3, 0) if (dy, dx) != (0, 0)]
    for dy, dx in row_offsets:
        pl.semaphore_signal(barrier, inc=1, device_id=(chip(dy, dx), col), device_id_type=MESH)
    for dz, dc in COL_ORDER:
        pl.semaphore_signal(barrier, inc=1, device_id=(row, column_of(dz, dc)), device_id_type=MESH)

    mine = pl.ds(row * 2, 2)
    first[32] = jnp.zeros_like(first[32])
    second[32] = jnp.zeros_like(second[32])
    for load in small:
        load.wait()
    for half in range(2):
        first[row * 2 + half] = start[:, half * 256 : (half + 1) * 256].astype(BF16)

    def forward(buf, turn, half, src, to, copies):
        (sy, sx), (ty, tx) = src, to
        piece = chip(SIDE - sy, SIDE - sx) * 2 + half
        arrives = ((sy + ty) % SIDE) * SIDE + (sx + tx) % SIDE
        copies.append(
            send(
                buf.at[piece], buf.at[piece], gather_s.at[turn, half, len(copies)], gather_r.at[turn, half, arrives],
                (chip(ty, tx), col),
            )
        )
        copies[-1].start()

    def turned(half, one, other):
        return (other, one) if half == 0 else (one, other)

    def gather_start(buf, turn, half):
        copies = []
        for d in NEAR_FAR:
            forward(buf, turn, half, (0, 0), turned(half, d, 0), copies)
        for d in NEAR_FAR:
            forward(buf, turn, half, (0, 0), turned(half, 0, d), copies)
        return copies

    def arrived(buf, turn, half, offset):
        dy, dx = offset
        piece = buf.at[chip(SIDE - dy, SIDE - dx) * 2 + half]
        send(
            piece, piece, gather_s.at[turn, half, 0], gather_r.at[turn, half, dy * SIDE + dx], (row, col)
        ).wait_recv()

    def gather_forward(buf, turn, half, copies, d):
        arrived(buf, turn, half, turned(half, d, 0))
        for e in NEAR_FAR:
            forward(buf, turn, half, turned(half, d, 0), turned(half, 0, e), copies)

    def gather_end(buf, turn, half, copies):
        for e in NEAR_FAR:
            for d in range(SIDE):
                arrived(buf, turn, half, turned(half, d, e))
        for copy in copies:
            copy.wait_send()

    gathers = []
    for i in range(block_rows):
        if i == 5:
            pl.semaphore_wait(barrier, len(row_offsets) + len(COL_ORDER))
            gathers = [gather_start(first, 0, half) for half in range(2)]
        loads[i].wait()
        total = jnp.zeros((8, 256), F32)
        for s in range(slots):
            alive = jnp.where(s < counts[0, i], 1.0, 0.0).astype(F32)
            block = stored[i * slots + s].T
            stored[i * slots + s] = block
            total += jnp.sum(jnp.abs(block).astype(F32).reshape(32, 8, 256), axis=0) * alive
        deg_out[i // 2, i % 2] = jnp.sum(total, axis=0, keepdims=True)

    deg_copies = []
    for k, (dz, dc) in enumerate(COL_ORDER):
        to = column_of(dz, dc)
        deg_copies.append(send(deg_out.at[to], deg_in.at[k], deg_s.at[k], deg_r.at[k], (row, to)))
        deg_copies[-1].start()
    for d in NEAR_FAR:
        for half in range(2):
            gather_forward(first, 0, half, gathers[half], d)
    degree = deg_out[col]
    for k, copy in enumerate(deg_copies):
        copy.wait_recv()
        degree = degree + deg_in[k]
    own_scale[...] = 1.0 / jnp.sqrt(degree)
    scales[mine] = own_scale[...]
    scale_copies = []
    for k, (dy, dx) in enumerate(row_offsets):
        scale_copies.append(send(own_scale, scales.at[mine], scale_s.at[k], scale_r.at[k], (chip(dy, dx), col)))
        scale_copies[-1].start()
    for half in range(2):
        gather_end(first, 0, half, gathers[half])
    for k, (dy, dx) in enumerate(row_offsets):
        theirs = pl.ds(chip(SIDE - dy, SIDE - dx) * 2, 2)
        send(own_scale, scales.at[theirs], scale_s.at[k], scale_r.at[k], (row, col)).wait_recv()

    def scale_block(g, carry):
        first[g] = (first[g].astype(F32) * scales[g]).astype(BF16)
        return carry

    lax.fori_loop(0, 32, scale_block, 0, unroll=4)

    def product(buf, turn, half):
        started = []
        for k, (dz, dc) in enumerate(COL_ORDER + ((0, 0),)):
            to = column_of(dz, dc)
            i = to * 2 + half
            total = jnp.zeros((64, 256), F32)
            for s in range(slots):
                g = jnp.where(s < counts[0, i], columns[s, i], 32)
                total += jnp.dot(buf[g], stored[i * slots + s], preferred_element_type=F32)
            if k == len(COL_ORDER):
                part_own[half] = total
            else:
                part_out[turn, half, k] = total.astype(BF16)
                started.append(
                    send(
                        part_out.at[turn, half, k], part_in.at[turn, half, k], part_s.at[turn, half, k],
                        part_r.at[turn, half, k], (row, to),
                    )
                )
                started[-1].start()
        return started

    def summed(started, turn, half):
        total = part_own[half]
        for k, copy in enumerate(started):
            copy.wait_recv()
            total = total + part_in[turn, half, k].astype(F32)
        return total * own_scale[half]

    def local_gram(values):
        return lax.dot_general(values, values, NT, precision=HIGHEST, preferred_element_type=F32)

    parts = [product(first, 0, half) for half in range(2)]
    gathers, gram = [], jnp.zeros((64, 64), F32)
    for half in range(2):
        values = summed(parts[half], 0, half)
        second[row * 2 + half] = (values * own_scale[half]).astype(BF16)
        gathers.append(gather_start(second, 1, half))
        gram += local_gram(values)
    sent = parts[0] + parts[1] + deg_copies + scale_copies
    packed = pack(gram)
    for p in range(8):
        piece_out[p] = packed[p * 4 : (p + 1) * 4]
    piece_copies = []
    for k, (dz, dc) in enumerate(COL_ORDER):
        to = column_of(dz, dc)
        piece_copies.append(send(piece_out.at[to], piece_in.at[k], pa_s.at[k], pa_r.at[k], (row, to)))
        piece_copies[-1].start()
    for d in NEAR_FAR:
        gather_forward(second, 1, 0, gathers[0], d)
    for d in NEAR_FAR:
        gather_forward(second, 1, 1, gathers[1], d)
    total = piece_out[col]
    for k, copy in enumerate(piece_copies):
        copy.wait_recv()
        total = total + piece_in[k]
    piece_sum[0] = total
    across = []
    for k, (dy, dx) in enumerate(row_offsets):
        across.append(send(piece_sum.at[0], piece_row.at[k], pb_s.at[k], pb_r.at[k], (chip(dy, dx), col)))
        across[-1].start()
    sent += piece_copies + across
    for half in range(2):
        gather_end(second, 1, half, gathers[half])

    parts = [product(second, 1, 0)]
    for k, copy in enumerate(across):
        copy.wait_recv()
        total = total + piece_row[k]
    piece_sum[1] = total
    piece_all[col] = total
    back = []
    for k, (dz, dc) in enumerate(COL_ORDER):
        back.append(send(piece_sum.at[1], piece_all.at[col], pc_s.at[k], pc_r.at[k], (row, column_of(dz, dc))))
        back[-1].start()
    parts.append(product(second, 1, 1))
    for k, (dz, dc) in enumerate(COL_ORDER):
        source = piece_all.at[column_of(SIDE - dz, dc)]
        send(source, source, pc_s.at[k], pc_r.at[k], (row, col)).wait_recv()
    inverse = inverse_factor(unpack(jnp.concatenate([piece_all[p] for p in range(8)], axis=0)) / sites)
    gram = jnp.zeros((64, 64), F32)
    for half in range(2):
        values = jnp.dot(inverse, summed(parts[half], 1, half), precision=HIGHEST, preferred_element_type=F32)
        grown[half] = values
        gram += local_gram(values)
    sent += back + parts[0] + parts[1]

    gram_out[...] = pack(gram).astype(BF16)
    group = []
    for k, (dz, dc) in enumerate(COL_ORDER):
        group.append(send(gram_out, gram_in.at[k], ga_s.at[k], ga_r.at[k], (row, column_of(dz, dc))))
        group[-1].start()
    total = gram_out[...].astype(F32)
    for k, copy in enumerate(group):
        copy.wait_recv()
        total = total + gram_in[k].astype(F32)
    cross_out[...] = total.astype(BF16)
    across = []
    for k, (dy, dx) in enumerate(row_offsets):
        across.append(send(cross_out, cross_in.at[k], gb_s.at[k], gb_r.at[k], (chip(dy, dx), col)))
        across[-1].start()
    for copy in sent + group:
        copy.wait_send()
    total = cross_out[...].astype(F32)
    for k, copy in enumerate(across):
        copy.wait_recv()
        total = total + cross_in[k].astype(F32)
    inverse = inverse_factor(unpack(total) / sites)
    for half in range(2):
        out[:, half * 256 : (half + 1) * 256] = jnp.dot(
            inverse, grown[half], precision=HIGHEST, preferred_element_type=F32
        )
    for copy in across:
        copy.wait_send()


def per_device(panel, blocks, columns, counts):
    dma = pltpu.SemaphoreType.DMA
    return pl.pallas_call(
        kernel,
        out_shape=jax.ShapeDtypeStruct(panel.shape, F32),
        in_specs=[pl.BlockSpec(memory_space=pl.ANY)] * 4,
        out_specs=pl.BlockSpec(memory_space=pltpu.VMEM),
        scratch_shapes=[
            pltpu.VMEM((128, 256, 256), BF16),
            pltpu.VMEM((64, 512), F32),
            pltpu.SMEM((8, 16), jnp.int32),
            pltpu.SMEM((1, 16), jnp.int32),
            pltpu.VMEM((33, 64, 256), BF16),
            pltpu.VMEM((33, 64, 256), BF16),
            pltpu.VMEM((32, 1, 256), F32),
            pltpu.VMEM((2, 1, 256), F32),
            pltpu.VMEM((8, 2, 1, 256), F32),
            pltpu.VMEM((7, 2, 1, 256), F32),
            pltpu.VMEM((2, 2, 7, 64, 256), BF16),
            pltpu.VMEM((2, 2, 7, 64, 256), BF16),
            pltpu.VMEM((2, 64, 256), F32),
            pltpu.VMEM((8, 4, 128), F32),
            pltpu.VMEM((7, 4, 128), F32),
            pltpu.VMEM((2, 4, 128), F32),
            pltpu.VMEM((15, 4, 128), F32),
            pltpu.VMEM((8, 4, 128), F32),
            pltpu.VMEM((32, 128), BF16),
            pltpu.VMEM((7, 32, 128), BF16),
            pltpu.VMEM((32, 128), BF16),
            pltpu.VMEM((15, 32, 128), BF16),
            pltpu.VMEM((2, 64, 256), F32),
            dma((3,)),
            dma((16,)),
            dma((7,)),
            dma((7,)),
            dma((15,)),
            dma((15,)),
            dma((2, 2, 15)),
            dma((2, 2, 16)),
            dma((2, 2, 7)),
            dma((2, 2, 7)),
            dma((7,)),
            dma((7,)),
            dma((15,)),
            dma((15,)),
            dma((7,)),
            dma((7,)),
            dma((7,)),
            dma((7,)),
            dma((15,)),
            dma((15,)),
        ],
        compiler_params=pltpu.CompilerParams(
            collective_id=0, has_side_effects=True, vmem_limit_bytes=48 * 2**20
        ),
    )(panel, blocks, jnp.transpose(columns, (1, 2, 0)), jnp.transpose(counts))


def solution(mesh):
    in_specs = (
        P(None, ("row", "col")),
        P("row", "col", None, None, None),
        P("row", "col", None),
        P("row", "col"),
    )
    return jax.shard_map(
        per_device, mesh=mesh, in_specs=in_specs, out_specs=P(None, ("row", "col")), check_vma=False
    )
```

time: 389 us -> 64.9 us (0.17)
  blocking collectives: 160 us -> 0 us
  waiting for transfers between devices: 142 us -> 0 us
  Pallas kernels: 0 us -> 61.8 us
  other arithmetic: 33.2 us -> 0 us
  matrix products: 27.9 us -> 0 us
  between operations: 13.9 us -> 0.01 us
  local copies, waits for them, and re-layouts: 11.3 us -> 2.9 us
    psum x2 -> x0, blocking collectives: 135 us -> none  [per_device(): gram = lax.psum(gram_local, ('row', 'col')) / total_sites]
    all_gather x2 -> x0, waiting for transfers between devices: 81.9 us -> none  [per_device(): whole = lax.all_gather(sent, 'row', axis=1, tiled=True)]
    pallas_call x0 -> x1, Pallas kernels: none -> 61.8 us  [per_device(): pl.pallas_call(kernel, out_shape=jax.ShapeDtypeStruct(panel.shape, F32),...]
    reduce_scatter x2 -> x0, waiting for transfers between devices: 60.1 us -> none  [per_device(): mine = lax.psum_scatter(prod, 'col', scatter_dimension=1, tiled=True)]
    unnamed x1 -> x0, blocking collectives: 24.9 us -> none
    dot_general x5 -> x0, matrix products: 24.2 us -> none  [the longest x2 21.5 us: per_device(): jnp.einsum('pbks,bkrs->pbr', picked, stored, preferred_element_type=jnp.f...]
    another operation x10 -> x0, other arithmetic: 24.1 us -> none  [the longest x6 13 us: per_device(): lower = jnp.linalg.cholesky(gram)]
    reduce_sum x1 -> x0, other arithmetic: 7.65 us -> none  [per_device(): jnp.einsum('bkrs,bk->br', jnp.abs(stored), alive, preferred_element_type=...]
  transfers between devices with their start and end apart: 4 -> 0, of which waited for: 4 -> 0; matrix products, arithmetic and copies ran while one was open for 0% -> 0% of each run, Pallas kernels for 0% -> 0%
where the time goes in v2:
time: 64.9 us; the launch traced here: 64.8 us
  Pallas kernels  61.8 us (95%)
  local copies, waits for them, and re-layouts  2.9 us (4%)
    pallas_call x1, Pallas kernels, per_device(): pl.pallas_call(kernel, out_shape=jax.ShapeDtypeStruct(panel.shape, F32),...  61.8 us
    unnamed x7, local copies, waits for them, and re-layouts  2.9 us

profile of v2, /device:TPU:1, one launch (start us, length us, event | category | flops | bytes accessed | tf_op | source)
XLA Modules:
  0.0 64.8 jit_solution(4982009540740841496)
XLA Ops:
  0.0 0.0 copy-start
  0.0 0.9 %copy-done = f32[64,512]{1,0:T(8,128)S(1)} copy-done((f32[64,512]{1,0:T(8,128)S(1)}, f32[64,512]{1,0:T(8,128)}, u32[]{:S(2)}) %copy-start) | copy-done | bytes 131096
  0.9 0.0 copy-start.1
  0.9 0.7 %copy-done.1 = s32[16,1,8]{0,2,1:T(8,128)S(1)} copy-done((s32[16,1,8]{0,2,1:T(8,128)S(1)}, s32[16,1,8]{0,2,1:T(8,128)}, u32[]{:S(2)}) %copy-start.1) | copy-done | bytes 536
  1.6 0.0 copy-start.2
  1.6 0.7 %copy-done.2 = s32[16,1]{0,1:T(1,128)S(1)} copy-done((s32[16,1]{0,1:T(1,128)S(1)}, s32[16,1]{0,1:T(1,128)}, u32[]{:S(2)}) %copy-start.2) | copy-done | bytes 88
  2.2 61.8 %shard_map.46 = f32[64,512]{1,0:T(8,128)S(1)} custom-call(f32[64,512]{1,0:T(8,128)S(1)} %copy-done, bf16[16,1,8,256,256]{4,3,2,1,0:T(8,128)(2,1)} %blocks.1, s32[1,8,16]{2,1,0:T(8,128)S(1)} %bitcast.2, s32[1,16]{1,0:T(1,128)S(1)} %bitcast.3), custom_call_target="tpu_custom_call" | custom-call | tf_op jit(solution)/shard_map/pallas_call | solution.py:309
  64.1 0.7 %copy.6 = f32[64,512]{1,0:T(8,128)} copy(f32[64,512]{1,0:T(8,128)S(1)} %shard_map.46) | data formatting | bytes 262144
Async XLA Ops:
  0.0 0.9 %copy-start = (f32[64,512]{1,0:T(8,128)S(1)}, f32[64,512]{1,0:T(8,128)}, u32[]{:S(2)}) copy-start(f32[64,512]{1,0:T(8,128)} %panel.1) | copy-start | bytes 393220
  0.9 0.7 %copy-start.1 = (s32[16,1,8]{0,2,1:T(8,128)S(1)}, s32[16,1,8]{0,2,1:T(8,128)}, u32[]{:S(2)}) copy-start(s32[16,1,8]{0,2,1:T(8,128)} %param.6) | copy-start | bytes 1540
  1.6 0.7 %copy-start.2 = (s32[16,1]{0,1:T(1,128)S(1)}, s32[16,1]{0,1:T(1,128)}, u32[]{:S(2)}) copy-start(s32[16,1]{0,1:T(1,128)} %param.7) | copy-start | bytes 196

commit v3 on v2

--- a/solution.py
+++ b/solution.py
@@ -13,9 +13,13 @@
 BF16 = jnp.bfloat16
 NT = (((1,), (1,)), ((), ()))
 SIDE = 4
+DEAD = 32
 PANEL = 16
 
-COL_ORDER = ((2, 0), (2, 1), (1, 0), (1, 1), (3, 0), (3, 1), (0, 1))
+COL_ORDER = ((2, 0), (2, 1), (1, 0), (1, 1), (3, 0), (3, 1), (0, 1), (0, 0))
+OTHERS = COL_ORDER[:-1]
+Z_ORDER = (2, 1, 3)
+FAR, NEAR = pl.ds(0, 3), pl.ds(3, 1)
 NEAR_FAR = (1, 3, 2)
 
 
@@ -52,16 +56,16 @@
 
 
 def kernel(
-    panel, blocks, columns_hbm, counts_hbm, out,
-    stored, start, columns, counts, first, second, scales, own_scale, deg_out, deg_in, part_out, part_in, part_own,
+    panel, blocks, table_in, out,
+    stored, start, table, first, second, scales, own_scale, deg_out, deg_in, pair_out, pair_in, far_out, far_in, part_own,
     piece_out, piece_in, piece_sum, piece_row, piece_all, gram_out, gram_in, cross_out, cross_in, grown,
-    small_sem, load_sem, deg_s, deg_r, scale_s, scale_r, gather_s, gather_r, part_s, part_r,
+    small_sem, load_sem, deg_s, deg_r, scale_s, scale_r, gather_s, gather_r, pair_s, pair_r, far_s, far_r,
     pa_s, pa_r, pb_s, pb_r, pc_s, pc_r, ga_s, ga_r, gb_s, gb_r,
 ):
     row, col = lax.axis_index("row"), lax.axis_index("col")
     y, x = row // SIDE, row % SIDE
     z, core = col // 2, col % 2
-    slots, block_rows = columns.shape
+    slots, block_rows = table.shape
     sites = 65536
 
     def chip(dy, dx):
@@ -75,10 +79,13 @@
             src_ref=src, dst_ref=dst, send_sem=send_sem, recv_sem=recv_sem, device_id=to, device_id_type=MESH
         )
 
+    def arrivals(copies):
+        for copy in copies:
+            copy.wait_recv()
+
     small = [
         pltpu.make_async_copy(panel, start, small_sem.at[0]),
-        pltpu.make_async_copy(counts_hbm, counts, small_sem.at[1]),
-        pltpu.make_async_copy(columns_hbm.at[0], columns, small_sem.at[2]),
+        pltpu.make_async_copy(table_in, table, small_sem.at[1]),
     ]
     loads = [
         pltpu.make_async_copy(blocks.at[i, 0], stored.at[pl.ds(i * slots, slots)], load_sem.at[i])
@@ -91,12 +98,12 @@
     row_offsets = [(dy, dx) for dy in (2, 1, 3, 0) for dx in (2, 1, 3, 0) if (dy, dx) != (0, 0)]
     for dy, dx in row_offsets:
         pl.semaphore_signal(barrier, inc=1, device_id=(chip(dy, dx), col), device_id_type=MESH)
-    for dz, dc in COL_ORDER:
+    for dz, dc in OTHERS:
         pl.semaphore_signal(barrier, inc=1, device_id=(row, column_of(dz, dc)), device_id_type=MESH)
 
     mine = pl.ds(row * 2, 2)
-    first[32] = jnp.zeros_like(first[32])
-    second[32] = jnp.zeros_like(second[32])
+    first[DEAD] = jnp.zeros_like(first[DEAD])
+    second[DEAD] = jnp.zeros_like(second[DEAD])
     for load in small:
         load.wait()
     for half in range(2):
@@ -147,29 +154,27 @@
     gathers = []
     for i in range(block_rows):
         if i == 5:
-            pl.semaphore_wait(barrier, len(row_offsets) + len(COL_ORDER))
+            pl.semaphore_wait(barrier, len(row_offsets) + len(OTHERS))
             gathers = [gather_start(first, 0, half) for half in range(2)]
         loads[i].wait()
         total = jnp.zeros((8, 256), F32)
         for s in range(slots):
-            alive = jnp.where(s < counts[0, i], 1.0, 0.0).astype(F32)
+            alive = jnp.where(table[s, i] < DEAD, 1.0, 0.0).astype(F32)
             block = stored[i * slots + s].T
             stored[i * slots + s] = block
             total += jnp.sum(jnp.abs(block).astype(F32).reshape(32, 8, 256), axis=0) * alive
         deg_out[i // 2, i % 2] = jnp.sum(total, axis=0, keepdims=True)
 
     deg_copies = []
-    for k, (dz, dc) in enumerate(COL_ORDER):
+    for k, (dz, dc) in enumerate(OTHERS):
         to = column_of(dz, dc)
         deg_copies.append(send(deg_out.at[to], deg_in.at[k], deg_s.at[k], deg_r.at[k], (row, to)))
         deg_copies[-1].start()
     for d in NEAR_FAR:
         for half in range(2):
             gather_forward(first, 0, half, gathers[half], d)
-    degree = deg_out[col]
-    for k, copy in enumerate(deg_copies):
-        copy.wait_recv()
-        degree = degree + deg_in[k]
+    arrivals(deg_copies)
+    degree = sum((deg_in[k] for k in range(7)), deg_out[col])
     own_scale[...] = 1.0 / jnp.sqrt(degree)
     scales[mine] = own_scale[...]
     scale_copies = []
@@ -188,51 +193,71 @@
 
     lax.fori_loop(0, 32, scale_block, 0, unroll=4)
 
-    def product(buf, turn, half):
-        started = []
-        for k, (dz, dc) in enumerate(COL_ORDER + ((0, 0),)):
-            to = column_of(dz, dc)
-            i = to * 2 + half
-            total = jnp.zeros((64, 256), F32)
-            for s in range(slots):
-                g = jnp.where(s < counts[0, i], columns[s, i], 32)
-                total += jnp.dot(buf[g], stored[i * slots + s], preferred_element_type=F32)
-            if k == len(COL_ORDER):
-                part_own[half] = total
-            else:
-                part_out[turn, half, k] = total.astype(BF16)
-                started.append(
+    def block_row(buf, i):
+        total = jnp.zeros((64, 256), F32)
+        for s in range(slots):
+            total += jnp.dot(buf[table[s, i]], stored[i * slots + s], preferred_element_type=F32)
+        return total
+
+    def row_group(buf, wanted):
+        return [block_row(buf, column_of(dz, dc) * 2 + half) for dz, dc, half in wanted]
+
+    def to_other_core(turn, half, which):
+        src, dst = pair_out.at[turn, half, which], pair_in.at[turn, half, which]
+        k = 0 if which == FAR else 1
+        copy = send(src, dst, pair_s.at[turn, half, k], pair_r.at[turn, half, k], (row, column_of(0, 1)))
+        copy.start()
+        return copy
+
+    def product(buf, turn):
+        pairs, fars = [], []
+        for half in range(2):
+            for k, total in enumerate(row_group(buf, [(dz, 1, half) for dz in Z_ORDER])):
+                pair_out[turn, half, k] = total.astype(BF16)
+            pairs.append(to_other_core(turn, half, FAR))
+            totals = row_group(buf, [(dz, 0, half) for dz in Z_ORDER])
+            pairs[half].wait_recv()
+            for k, total in enumerate(totals):
+                far_out[turn, half, k] = (total + pair_in[turn, half, k].astype(F32)).astype(BF16)
+            fars.append([])
+            for k, dz in enumerate(Z_ORDER):
+                fars[half].append(
                     send(
-                        part_out.at[turn, half, k], part_in.at[turn, half, k], part_s.at[turn, half, k],
-                        part_r.at[turn, half, k], (row, to),
+                        far_out.at[turn, half, k], far_in.at[turn, half, k], far_s.at[turn, half, k],
+                        far_r.at[turn, half, k], (row, column_of(dz, 0)),
                     )
                 )
-                started[-1].start()
-        return started
+                fars[half][-1].start()
+        totals = row_group(buf, [(0, 1, 0), (0, 1, 1), (0, 0, 0), (0, 0, 1)])
+        for half in range(2):
+            pair_out[turn, half, len(Z_ORDER)] = totals[half].astype(BF16)
+            part_own[half] = totals[2 + half]
+        near = [to_other_core(turn, half, NEAR) for half in range(2)]
+        return [[near[half]] + fars[half] for half in range(2)], pairs + near + fars[0] + fars[1]
 
     def summed(started, turn, half):
-        total = part_own[half]
-        for k, copy in enumerate(started):
-            copy.wait_recv()
-            total = total + part_in[turn, half, k].astype(F32)
+        arrivals(started[half])
+        total = part_own[half] + pair_in[turn, half, len(Z_ORDER)].astype(F32)
+        for k in range(len(Z_ORDER)):
+            total += far_in[turn, half, k].astype(F32)
         return total * own_scale[half]
 
     def local_gram(values):
         return lax.dot_general(values, values, NT, precision=HIGHEST, preferred_element_type=F32)
 
-    parts = [product(first, 0, half) for half in range(2)]
+    parts, started = product(first, 0)
     gathers, gram = [], jnp.zeros((64, 64), F32)
     for half in range(2):
-        values = summed(parts[half], 0, half)
+        values = summed(parts, 0, half)
         second[row * 2 + half] = (values * own_scale[half]).astype(BF16)
         gathers.append(gather_start(second, 1, half))
         gram += local_gram(values)
-    sent = parts[0] + parts[1] + deg_copies + scale_copies
+    sent = started + deg_copies + scale_copies
     packed = pack(gram)
     for p in range(8):
         piece_out[p] = packed[p * 4 : (p + 1) * 4]
     piece_copies = []
-    for k, (dz, dc) in enumerate(COL_ORDER):
+    for k, (dz, dc) in enumerate(OTHERS):
         to = column_of(dz, dc)
         piece_copies.append(send(piece_out.at[to], piece_in.at[k], pa_s.at[k], pa_r.at[k], (row, to)))
         piece_copies[-1].start()
@@ -240,11 +265,8 @@
         gather_forward(second, 1, 0, gathers[0], d)
     for d in NEAR_FAR:
         gather_forward(second, 1, 1, gathers[1], d)
-    total = piece_out[col]
-    for k, copy in enumerate(piece_copies):
-        copy.wait_recv()
-        total = total + piece_in[k]
-    piece_sum[0] = total
+    arrivals(piece_copies)
+    piece_sum[0] = sum((piece_in[k] for k in range(7)), piece_out[col])
     across = []
     for k, (dy, dx) in enumerate(row_offsets):
         across.append(send(piece_sum.at[0], piece_row.at[k], pb_s.at[k], pb_r.at[k], (chip(dy, dx), col)))
@@ -253,37 +275,33 @@
     for half in range(2):
         gather_end(second, 1, half, gathers[half])
 
-    parts = [product(second, 1, 0)]
-    for k, copy in enumerate(across):
-        copy.wait_recv()
-        total = total + piece_row[k]
+    arrivals(across)
+    total = sum((piece_row[k] for k in range(15)), piece_sum[0])
     piece_sum[1] = total
     piece_all[col] = total
     back = []
-    for k, (dz, dc) in enumerate(COL_ORDER):
+    for k, (dz, dc) in enumerate(OTHERS):
         back.append(send(piece_sum.at[1], piece_all.at[col], pc_s.at[k], pc_r.at[k], (row, column_of(dz, dc))))
         back[-1].start()
-    parts.append(product(second, 1, 1))
-    for k, (dz, dc) in enumerate(COL_ORDER):
+    parts, started = product(second, 1)
+    for k, (dz, dc) in enumerate(OTHERS):
         source = piece_all.at[column_of(SIDE - dz, dc)]
         send(source, source, pc_s.at[k], pc_r.at[k], (row, col)).wait_recv()
     inverse = inverse_factor(unpack(jnp.concatenate([piece_all[p] for p in range(8)], axis=0)) / sites)
     gram = jnp.zeros((64, 64), F32)
     for half in range(2):
-        values = jnp.dot(inverse, summed(parts[half], 1, half), precision=HIGHEST, preferred_element_type=F32)
+        values = jnp.dot(inverse, summed(parts, 1, half), precision=HIGHEST, preferred_element_type=F32)
         grown[half] = values
         gram += local_gram(values)
-    sent += back + parts[0] + parts[1]
+    sent += back + started
 
     gram_out[...] = pack(gram).astype(BF16)
     group = []
-    for k, (dz, dc) in enumerate(COL_ORDER):
+    for k, (dz, dc) in enumerate(OTHERS):
         group.append(send(gram_out, gram_in.at[k], ga_s.at[k], ga_r.at[k], (row, column_of(dz, dc))))
         group[-1].start()
-    total = gram_out[...].astype(F32)
-    for k, copy in enumerate(group):
-        copy.wait_recv()
-        total = total + gram_in[k].astype(F32)
+    arrivals(group)
+    total = sum((gram_in[k].astype(F32) for k in range(7)), gram_out[...].astype(F32))
     cross_out[...] = total.astype(BF16)
     across = []
     for k, (dy, dx) in enumerate(row_offsets):
@@ -291,10 +309,8 @@
         across[-1].start()
     for copy in sent + group:
         copy.wait_send()
-    total = cross_out[...].astype(F32)
-    for k, copy in enumerate(across):
-        copy.wait_recv()
-        total = total + cross_in[k].astype(F32)
+    arrivals(across)
+    total = sum((cross_in[k].astype(F32) for k in range(15)), cross_out[...].astype(F32))
     inverse = inverse_factor(unpack(total) / sites)
     for half in range(2):
         out[:, half * 256 : (half + 1) * 256] = jnp.dot(
@@ -305,25 +321,28 @@
 
 
 def per_device(panel, blocks, columns, counts):
+    live = jnp.arange(columns.shape[2], dtype=jnp.int32)[:, None] < jnp.transpose(counts)
+    table = jnp.where(live, jnp.transpose(columns[:, 0]), DEAD)
     dma = pltpu.SemaphoreType.DMA
     return pl.pallas_call(
         kernel,
         out_shape=jax.ShapeDtypeStruct(panel.shape, F32),
-        in_specs=[pl.BlockSpec(memory_space=pl.ANY)] * 4,
+        in_specs=[pl.BlockSpec(memory_space=pl.ANY)] * 3,
         out_specs=pl.BlockSpec(memory_space=pltpu.VMEM),
         scratch_shapes=[
             pltpu.VMEM((128, 256, 256), BF16),
             pltpu.VMEM((64, 512), F32),
             pltpu.SMEM((8, 16), jnp.int32),
-            pltpu.SMEM((1, 16), jnp.int32),
             pltpu.VMEM((33, 64, 256), BF16),
             pltpu.VMEM((33, 64, 256), BF16),
             pltpu.VMEM((32, 1, 256), F32),
             pltpu.VMEM((2, 1, 256), F32),
             pltpu.VMEM((8, 2, 1, 256), F32),
             pltpu.VMEM((7, 2, 1, 256), F32),
-            pltpu.VMEM((2, 2, 7, 64, 256), BF16),
-            pltpu.VMEM((2, 2, 7, 64, 256), BF16),
+            pltpu.VMEM((2, 2, 4, 64, 256), BF16),
+            pltpu.VMEM((2, 2, 4, 64, 256), BF16),
+            pltpu.VMEM((2, 2, 3, 64, 256), BF16),
+            pltpu.VMEM((2, 2, 3, 64, 256), BF16),
             pltpu.VMEM((2, 64, 256), F32),
             pltpu.VMEM((8, 4, 128), F32),
             pltpu.VMEM((7, 4, 128), F32),
@@ -335,7 +354,7 @@
             pltpu.VMEM((32, 128), BF16),
             pltpu.VMEM((15, 32, 128), BF16),
             pltpu.VMEM((2, 64, 256), F32),
-            dma((3,)),
+            dma((2,)),
             dma((16,)),
             dma((7,)),
             dma((7,)),
@@ -343,8 +362,10 @@
             dma((15,)),
             dma((2, 2, 15)),
             dma((2, 2, 16)),
-            dma((2, 2, 7)),
-            dma((2, 2, 7)),
+            dma((2, 2, 2)),
+            dma((2, 2, 2)),
+            dma((2, 2, 3)),
+            dma((2, 2, 3)),
             dma((7,)),
             dma((7,)),
             dma((15,)),
@@ -359,7 +380,7 @@
         compiler_params=pltpu.CompilerParams(
             collective_id=0, has_side_effects=True, vmem_limit_bytes=48 * 2**20
         ),
-    )(panel, blocks, jnp.transpose(columns, (1, 2, 0)), jnp.transpose(counts))
+    )(panel, blocks, table)
 
 
 def solution(mesh):

time: 64.9 us -> 62.7 us (0.966)
  Pallas kernels: 61.8 us -> 60.2 us
  local copies, waits for them, and re-layouts: 2.9 us -> 1.56 us
  other arithmetic: 0 us -> 0.69 us
    pallas_call x1, Pallas kernels: 61.8 us -> 60.2 us  [per_device(): pl.pallas_call(kernel, out_shape=jax.ShapeDtypeStruct(panel.shape, F32),...]
    unnamed x7 -> x3, local copies, waits for them, and re-layouts: 2.9 us -> 1.56 us
    select_n x0 -> x1, other arithmetic: none -> 0.69 us  [per_device(): table = jnp.where(live, jnp.transpose(columns[:, 0]), DEAD)]
where the time goes in v3:
time: 62.7 us; the launch traced here: 62.5 us
  Pallas kernels  60.2 us (96%)
  local copies, waits for them, and re-layouts  1.56 us (2%)
  other arithmetic  0.69 us (1%)
    pallas_call x1, Pallas kernels, per_device(): pl.pallas_call(kernel, out_shape=jax.ShapeDtypeStruct(panel.shape, F32),...  60.2 us
    unnamed x3, local copies, waits for them, and re-layouts  1.56 us

profile of v3, /device:TPU:1, one launch (start us, length us, event | category | flops | bytes accessed | tf_op | source)
XLA Modules:
  0.0 62.5 jit_solution(2989955066443946186)
XLA Ops:
  0.0 0.7 %bitcast_select_fusion.table_in = s32[8,16]{1,0:T(8,128)S(1)} fusion(s32[16,1,8]{0,2,1:T(8,128)} %param.6, s32[16]{0:T(128)} %bitcast.5), kind=kLoop, calls=%fused_computation | loop fusion | flops 256 | bytes 1088 | tf_op jit(solution)/shard_map/jit(_where)/select_n | solution.py:325
  0.7 0.0 copy-start
  0.7 0.9 %copy-done = f32[64,512]{1,0:T(8,128)S(1)} copy-done((f32[64,512]{1,0:T(8,128)S(1)}, f32[64,512]{1,0:T(8,128)}, u32[]{:S(2)}) %copy-start) | copy-done | bytes 131096
  1.6 60.2 %shard_map.46 = f32[64,512]{1,0:T(8,128)S(1)} custom-call(f32[64,512]{1,0:T(8,128)S(1)} %copy-done, bf16[16,1,8,256,256]{4,3,2,1,0:T(8,128)(2,1)} %blocks.1, s32[8,16]{1,0:T(8,128)S(1)} %bitcast_select_fusion.table_in), custom_call_target="tpu_custom_call" | custom-call | tf_op jit(solution)/shard_map/pallas_call | solution.py:327
  61.9 0.7 %copy.6 = f32[64,512]{1,0:T(8,128)} copy(f32[64,512]{1,0:T(8,128)S(1)} %shard_map.46) | data formatting | bytes 262144
Async XLA Ops:
  0.7 0.9 %copy-start = (f32[64,512]{1,0:T(8,128)S(1)}, f32[64,512]{1,0:T(8,128)}, u32[]{:S(2)}) copy-start(f32[64,512]{1,0:T(8,128)} %panel.1) | copy-start | bytes 393220

commit v4 on v3

--- a/solution.py
+++ b/solution.py
@@ -21,6 +21,7 @@
 Z_ORDER = (2, 1, 3)
 FAR, NEAR = pl.ds(0, 3), pl.ds(3, 1)
 NEAR_FAR = (1, 3, 2)
+PARTS = (1, 2)
 
 
 def inverse_factor(gram):
@@ -58,9 +59,9 @@
 def kernel(
     panel, blocks, table_in, out,
     stored, start, table, first, second, scales, own_scale, deg_out, deg_in, pair_out, pair_in, far_out, far_in, part_own,
-    piece_out, piece_in, piece_sum, piece_row, piece_all, gram_out, gram_in, cross_out, cross_in, grown,
+    gram_out, gram_in, cross_out, cross_in, grown,
     small_sem, load_sem, deg_s, deg_r, scale_s, scale_r, gather_s, gather_r, pair_s, pair_r, far_s, far_r,
-    pa_s, pa_r, pb_s, pb_r, pc_s, pc_r, ga_s, ga_r, gb_s, gb_r,
+    ga_s, ga_r, gb_s, gb_r,
 ):
     row, col = lax.axis_index("row"), lax.axis_index("col")
     y, x = row // SIDE, row % SIDE
@@ -109,45 +110,54 @@
     for half in range(2):
         first[row * 2 + half] = start[:, half * 256 : (half + 1) * 256].astype(BF16)
 
-    def forward(buf, turn, half, src, to, copies):
+    def vectors(turn, part):
+        size = 64 // PARTS[turn]
+        return pl.ds(part * size, size)
+
+    def forward(buf, turn, half, part, src, to, copies):
         (sy, sx), (ty, tx) = src, to
-        piece = chip(SIDE - sy, SIDE - sx) * 2 + half
+        piece = buf.at[chip(SIDE - sy, SIDE - sx) * 2 + half, vectors(turn, part)]
         arrives = ((sy + ty) % SIDE) * SIDE + (sx + tx) % SIDE
         copies.append(
             send(
-                buf.at[piece], buf.at[piece], gather_s.at[turn, half, len(copies)], gather_r.at[turn, half, arrives],
+                piece, piece, gather_s.at[turn, half, len(copies)], gather_r.at[turn, half, part, arrives],
                 (chip(ty, tx), col),
             )
         )
         copies[-1].start()
 
-    def turned(half, one, other):
-        return (other, one) if half == 0 else (one, other)
+    def turned(turn, half, part, one, other):
+        along_x = half == 0 if PARTS[turn] == 1 else part % 2 == 0
+        return (other, one) if along_x else (one, other)
 
     def gather_start(buf, turn, half):
         copies = []
         for d in NEAR_FAR:
-            forward(buf, turn, half, (0, 0), turned(half, d, 0), copies)
+            for part in range(PARTS[turn]):
+                forward(buf, turn, half, part, (0, 0), turned(turn, half, part, d, 0), copies)
         for d in NEAR_FAR:
-            forward(buf, turn, half, (0, 0), turned(half, 0, d), copies)
+            for part in range(PARTS[turn]):
+                forward(buf, turn, half, part, (0, 0), turned(turn, half, part, 0, d), copies)
         return copies
 
-    def arrived(buf, turn, half, offset):
+    def arrived(buf, turn, half, part, offset):
         dy, dx = offset
-        piece = buf.at[chip(SIDE - dy, SIDE - dx) * 2 + half]
+        piece = buf.at[chip(SIDE - dy, SIDE - dx) * 2 + half, vectors(turn, part)]
         send(
-            piece, piece, gather_s.at[turn, half, 0], gather_r.at[turn, half, dy * SIDE + dx], (row, col)
+            piece, piece, gather_s.at[turn, half, 0], gather_r.at[turn, half, part, dy * SIDE + dx], (row, col)
         ).wait_recv()
 
     def gather_forward(buf, turn, half, copies, d):
-        arrived(buf, turn, half, turned(half, d, 0))
-        for e in NEAR_FAR:
-            forward(buf, turn, half, turned(half, d, 0), turned(half, 0, e), copies)
+        for part in range(PARTS[turn]):
+            arrived(buf, turn, half, part, turned(turn, half, part, d, 0))
+            for e in NEAR_FAR:
+                forward(buf, turn, half, part, turned(turn, half, part, d, 0), turned(turn, half, part, 0, e), copies)
 
     def gather_end(buf, turn, half, copies):
         for e in NEAR_FAR:
             for d in range(SIDE):
-                arrived(buf, turn, half, turned(half, d, e))
+                for part in range(PARTS[turn]):
+                    arrived(buf, turn, half, part, turned(turn, half, part, d, e))
         for copy in copies:
             copy.wait_send()
 
@@ -245,6 +255,36 @@
     def local_gram(values):
         return lax.dot_general(values, values, NT, precision=HIGHEST, preferred_element_type=F32)
 
+    def gram_to_group(gram, turn):
+        gram_out[turn] = pack(gram).astype(BF16)
+        copies = []
+        for k, (dz, dc) in enumerate(OTHERS):
+            copies.append(
+                send(
+                    gram_out.at[turn], gram_in.at[turn, k], ga_s.at[turn, k], ga_r.at[turn, k],
+                    (row, column_of(dz, dc)),
+                )
+            )
+            copies[-1].start()
+        return copies
+
+    def gram_across(group, turn):
+        arrivals(group)
+        total = sum((gram_in[turn, k].astype(F32) for k in range(7)), gram_out[turn].astype(F32))
+        cross_out[turn] = total.astype(BF16)
+        copies = []
+        for k, (dy, dx) in enumerate(row_offsets):
+            copies.append(
+                send(cross_out.at[turn], cross_in.at[turn, k], gb_s.at[turn, k], gb_r.at[turn, k], (chip(dy, dx), col))
+            )
+            copies[-1].start()
+        return copies
+
+    def gram_factor(across, turn):
+        arrivals(across)
+        total = sum((cross_in[turn, k].astype(F32) for k in range(15)), cross_out[turn].astype(F32))
+        return inverse_factor(unpack(total) / sites)
+
     parts, started = product(first, 0)
     gathers, gram = [], jnp.zeros((64, 64), F32)
     for half in range(2):
@@ -253,65 +293,32 @@
         gathers.append(gather_start(second, 1, half))
         gram += local_gram(values)
     sent = started + deg_copies + scale_copies
-    packed = pack(gram)
-    for p in range(8):
-        piece_out[p] = packed[p * 4 : (p + 1) * 4]
-    piece_copies = []
-    for k, (dz, dc) in enumerate(OTHERS):
-        to = column_of(dz, dc)
-        piece_copies.append(send(piece_out.at[to], piece_in.at[k], pa_s.at[k], pa_r.at[k], (row, to)))
-        piece_copies[-1].start()
-    for d in NEAR_FAR:
-        gather_forward(second, 1, 0, gathers[0], d)
-    for d in NEAR_FAR:
-        gather_forward(second, 1, 1, gathers[1], d)
-    arrivals(piece_copies)
-    piece_sum[0] = sum((piece_in[k] for k in range(7)), piece_out[col])
-    across = []
-    for k, (dy, dx) in enumerate(row_offsets):
-        across.append(send(piece_sum.at[0], piece_row.at[k], pb_s.at[k], pb_r.at[k], (chip(dy, dx), col)))
-        across[-1].start()
-    sent += piece_copies + across
+    group = gram_to_group(gram, 0)
+    gather_forward(second, 1, 0, gathers[0], NEAR_FAR[0])
+    gather_forward(second, 1, 0, gathers[0], NEAR_FAR[1])
+    gather_forward(second, 1, 1, gathers[1], NEAR_FAR[0])
+    gather_forward(second, 1, 0, gathers[0], NEAR_FAR[2])
+    gather_forward(second, 1, 1, gathers[1], NEAR_FAR[1])
+    gather_forward(second, 1, 1, gathers[1], NEAR_FAR[2])
     for half in range(2):
         gather_end(second, 1, half, gathers[half])
-
-    arrivals(across)
-    total = sum((piece_row[k] for k in range(15)), piece_sum[0])
-    piece_sum[1] = total
-    piece_all[col] = total
-    back = []
-    for k, (dz, dc) in enumerate(OTHERS):
-        back.append(send(piece_sum.at[1], piece_all.at[col], pc_s.at[k], pc_r.at[k], (row, column_of(dz, dc))))
-        back[-1].start()
+    across = gram_across(group, 0)
+    sent += group + across
+
     parts, started = product(second, 1)
-    for k, (dz, dc) in enumerate(OTHERS):
-        source = piece_all.at[column_of(SIDE - dz, dc)]
-        send(source, source, pc_s.at[k], pc_r.at[k], (row, col)).wait_recv()
-    inverse = inverse_factor(unpack(jnp.concatenate([piece_all[p] for p in range(8)], axis=0)) / sites)
+    inverse = gram_factor(across, 0)
     gram = jnp.zeros((64, 64), F32)
     for half in range(2):
         values = jnp.dot(inverse, summed(parts, 1, half), precision=HIGHEST, preferred_element_type=F32)
         grown[half] = values
         gram += local_gram(values)
-    sent += back + started
-
-    gram_out[...] = pack(gram).astype(BF16)
-    group = []
-    for k, (dz, dc) in enumerate(OTHERS):
-        group.append(send(gram_out, gram_in.at[k], ga_s.at[k], ga_r.at[k], (row, column_of(dz, dc))))
-        group[-1].start()
-    arrivals(group)
-    total = sum((gram_in[k].astype(F32) for k in range(7)), gram_out[...].astype(F32))
-    cross_out[...] = total.astype(BF16)
-    across = []
-    for k, (dy, dx) in enumerate(row_offsets):
-        across.append(send(cross_out, cross_in.at[k], gb_s.at[k], gb_r.at[k], (chip(dy, dx), col)))
-        across[-1].start()
+    sent += started
+
+    group = gram_to_group(gram, 1)
+    across = gram_across(group, 1)
     for copy in sent + group:
         copy.wait_send()
-    arrivals(across)
-    total = sum((cross_in[k].astype(F32) for k in range(15)), cross_out[...].astype(F32))
-    inverse = inverse_factor(unpack(total) / sites)
+    inverse = gram_factor(across, 1)
     for half in range(2):
         out[:, half * 256 : (half + 1) * 256] = jnp.dot(
             inverse, grown[half], precision=HIGHEST, preferred_element_type=F32
@@ -344,15 +351,10 @@
             pltpu.VMEM((2, 2, 3, 64, 256), BF16),
             pltpu.VMEM((2, 2, 3, 64, 256), BF16),
             pltpu.VMEM((2, 64, 256), F32),
-            pltpu.VMEM((8, 4, 128), F32),
-            pltpu.VMEM((7, 4, 128), F32),
-            pltpu.VMEM((2, 4, 128), F32),
-            pltpu.VMEM((15, 4, 128), F32),
-            pltpu.VMEM((8, 4, 128), F32),
-            pltpu.VMEM((32, 128), BF16),
-            pltpu.VMEM((7, 32, 128), BF16),
-            pltpu.VMEM((32, 128), BF16),
-            pltpu.VMEM((15, 32, 128), BF16),
+            pltpu.VMEM((2, 32, 128), BF16),
+            pltpu.VMEM((2, 7, 32, 128), BF16),
+            pltpu.VMEM((2, 32, 128), BF16),
+            pltpu.VMEM((2, 15, 32, 128), BF16),
             pltpu.VMEM((2, 64, 256), F32),
             dma((2,)),
             dma((16,)),
@@ -360,22 +362,16 @@
             dma((7,)),
             dma((15,)),
             dma((15,)),
-            dma((2, 2, 15)),
-            dma((2, 2, 16)),
+            dma((2, 2, 30)),
+            dma((2, 2, 2, 16)),
             dma((2, 2, 2)),
             dma((2, 2, 2)),
             dma((2, 2, 3)),
             dma((2, 2, 3)),
-            dma((7,)),
-            dma((7,)),
-            dma((15,)),
-            dma((15,)),
-            dma((7,)),
-            dma((7,)),
-            dma((7,)),
-            dma((7,)),
-            dma((15,)),
-            dma((15,)),
+            dma((2, 7)),
+            dma((2, 7)),
+            dma((2, 15)),
+            dma((2, 15)),
         ],
         compiler_params=pltpu.CompilerParams(
             collective_id=0, has_side_effects=True, vmem_limit_bytes=48 * 2**20

time: 62.7 us -> 61 us (0.973)
  Pallas kernels: 60.2 us -> 58.6 us
    pallas_call x1, Pallas kernels: 60.2 us -> 58.6 us  [per_device(): pl.pallas_call(kernel, out_shape=jax.ShapeDtypeStruct(panel.shape, F32),...]
where the time goes in v4:
time: 61 us; the launch traced here: 60.8 us
  Pallas kernels  58.6 us (96%)
  local copies, waits for them, and re-layouts  1.56 us (3%)
  other arithmetic  0.69 us (1%)
    pallas_call x1, Pallas kernels, per_device(): pl.pallas_call(kernel, out_shape=jax.ShapeDtypeStruct(panel.shape, F32),...  58.6 us
    unnamed x3, local copies, waits for them, and re-layouts  1.56 us

profile of v4, /device:TPU:1, one launch (start us, length us, event | category | flops | bytes accessed | tf_op | source)
XLA Modules:
  0.0 60.8 jit_solution(15838275296674139759)
XLA Ops:
  0.0 0.7 %bitcast_select_fusion.table_in = s32[8,16]{1,0:T(8,128)S(1)} fusion(s32[16,1,8]{0,2,1:T(8,128)} %param.6, s32[16]{0:T(128)} %bitcast.5), kind=kLoop, calls=%fused_computation | loop fusion | flops 256 | bytes 1088 | tf_op jit(solution)/shard_map/jit(_where)/select_n | solution.py:332
  0.7 0.0 copy-start
  0.7 0.9 %copy-done = f32[64,512]{1,0:T(8,128)S(1)} copy-done((f32[64,512]{1,0:T(8,128)S(1)}, f32[64,512]{1,0:T(8,128)}, u32[]{:S(2)}) %copy-start) | copy-done | bytes 131096
  1.6 58.6 %shard_map.46 = f32[64,512]{1,0:T(8,128)S(1)} custom-call(f32[64,512]{1,0:T(8,128)S(1)} %copy-done, bf16[16,1,8,256,256]{4,3,2,1,0:T(8,128)(2,1)} %blocks.1, s32[8,16]{1,0:T(8,128)S(1)} %bitcast_select_fusion.table_in), custom_call_target="tpu_custom_call" | custom-call | tf_op jit(solution)/shard_map/pallas_call | solution.py:334
  60.2 0.7 %copy.6 = f32[64,512]{1,0:T(8,128)} copy(f32[64,512]{1,0:T(8,128)S(1)} %shard_map.46) | data formatting | bytes 262144
Async XLA Ops:
  0.7 0.9 %copy-start = (f32[64,512]{1,0:T(8,128)S(1)}, f32[64,512]{1,0:T(8,128)}, u32[]{:S(2)}) copy-start(f32[64,512]{1,0:T(8,128)} %panel.1) | copy-start | bytes 393220

commit v5 on v4

--- a/solution.py
+++ b/solution.py
@@ -13,6 +13,7 @@
 BF16 = jnp.bfloat16
 NT = (((1,), (1,)), ((), ()))
 SIDE = 4
+ENTRY = 5
 DEAD = 32
 PANEL = 16
 
@@ -66,7 +67,7 @@
     row, col = lax.axis_index("row"), lax.axis_index("col")
     y, x = row // SIDE, row % SIDE
     z, core = col // 2, col % 2
-    slots, block_rows = table.shape
+    slots = table.shape[0]
     sites = 65536
 
     def chip(dy, dx):
@@ -88,9 +89,10 @@
         pltpu.make_async_copy(panel, start, small_sem.at[0]),
         pltpu.make_async_copy(table_in, table, small_sem.at[1]),
     ]
+    by_owner = [column_of(dz, dc) * 2 + half for dz, dc in COL_ORDER for half in range(2)]
     loads = [
-        pltpu.make_async_copy(blocks.at[i, 0], stored.at[pl.ds(i * slots, slots)], load_sem.at[i])
-        for i in range(block_rows)
+        pltpu.make_async_copy(blocks.at[i, 0], stored.at[pl.ds(i * slots, slots)], load_sem.at[n])
+        for n, i in enumerate(by_owner)
     ]
     for load in small + loads:
         load.start()
@@ -161,36 +163,43 @@
         for copy in copies:
             copy.wait_send()
 
-    gathers = []
-    for i in range(block_rows):
-        if i == 5:
+    gathers, deg_copies, begun = [], [], 0
+    for n, i in enumerate(by_owner):
+        if n == ENTRY:
             pl.semaphore_wait(barrier, len(row_offsets) + len(OTHERS))
             gathers = [gather_start(first, 0, half) for half in range(2)]
-        loads[i].wait()
+        loads[n].wait()
         total = jnp.zeros((8, 256), F32)
         for s in range(slots):
             alive = jnp.where(table[s, i] < DEAD, 1.0, 0.0).astype(F32)
             block = stored[i * slots + s].T
             stored[i * slots + s] = block
             total += jnp.sum(jnp.abs(block).astype(F32).reshape(32, 8, 256), axis=0) * alive
-        deg_out[i // 2, i % 2] = jnp.sum(total, axis=0, keepdims=True)
-
-    deg_copies = []
-    for k, (dz, dc) in enumerate(OTHERS):
-        to = column_of(dz, dc)
-        deg_copies.append(send(deg_out.at[to], deg_in.at[k], deg_s.at[k], deg_r.at[k], (row, to)))
-        deg_copies[-1].start()
-    for d in NEAR_FAR:
+        deg_out[n // 2, n % 2] = jnp.sum(total, axis=0, keepdims=True)
+        if n % 2 == 1 and n // 2 < len(OTHERS):
+            k = n // 2
+            deg_copies.append(
+                send(deg_out.at[k], deg_in.at[k], deg_s.at[k], deg_r.at[k], (row, column_of(*COL_ORDER[k])))
+            )
+        if n >= ENTRY:
+            for copy in deg_copies[begun:]:
+                copy.start()
+            begun = len(deg_copies)
+
+    for d in NEAR_FAR[:2]:
         for half in range(2):
             gather_forward(first, 0, half, gathers[half], d)
     arrivals(deg_copies)
-    degree = sum((deg_in[k] for k in range(7)), deg_out[col])
+    degree = sum((deg_in[k] for k in range(7)), deg_out[7])
     own_scale[...] = 1.0 / jnp.sqrt(degree)
     scales[mine] = own_scale[...]
     scale_copies = []
     for k, (dy, dx) in enumerate(row_offsets):
         scale_copies.append(send(own_scale, scales.at[mine], scale_s.at[k], scale_r.at[k], (chip(dy, dx), col)))
         scale_copies[-1].start()
+    for d in NEAR_FAR[2:]:
+        for half in range(2):
+            gather_forward(first, 0, half, gathers[half], d)
     for half in range(2):
         gather_end(first, 0, half, gathers[half])
     for k, (dy, dx) in enumerate(row_offsets):

time: 61 us -> 60.4 us (level)
  Pallas kernels: 58.6 us -> 57.9 us
    pallas_call x1, Pallas kernels: 58.6 us -> 57.9 us  [per_device(): pl.pallas_call(kernel, out_shape=jax.ShapeDtypeStruct(panel.shape, F32),...]
where the time goes in v5:
time: 60.4 us; the launch traced here: 60.2 us
  Pallas kernels  57.9 us (96%)
  local copies, waits for them, and re-layouts  1.56 us (3%)
  other arithmetic  0.69 us (1%)
    pallas_call x1, Pallas kernels, per_device(): pl.pallas_call(kernel, out_shape=jax.ShapeDtypeStruct(panel.shape, F32),...  57.9 us
    unnamed x3, local copies, waits for them, and re-layouts  1.56 us

profile of v5, /device:TPU:1, one launch (start us, length us, event | category | flops | bytes accessed | tf_op | source)
XLA Modules:
  0.0 60.2 jit_solution(7390181977092298098)
XLA Ops:
  0.0 0.7 %bitcast_select_fusion.table_in = s32[8,16]{1,0:T(8,128)S(1)} fusion(s32[16,1,8]{0,2,1:T(8,128)} %param.6, s32[16]{0:T(128)} %bitcast.5), kind=kLoop, calls=%fused_computation | loop fusion | flops 256 | bytes 1088 | tf_op jit(solution)/shard_map/jit(_where)/select_n | solution.py:341
  0.7 0.0 copy-start
  0.7 0.9 %copy-done = f32[64,512]{1,0:T(8,128)S(1)} copy-done((f32[64,512]{1,0:T(8,128)S(1)}, f32[64,512]{1,0:T(8,128)}, u32[]{:S(2)}) %copy-start) | copy-done | bytes 131096
  1.6 57.9 %shard_map.46 = f32[64,512]{1,0:T(8,128)S(1)} custom-call(f32[64,512]{1,0:T(8,128)S(1)} %copy-done, bf16[16,1,8,256,256]{4,3,2,1,0:T(8,128)(2,1)} %blocks.1, s32[8,16]{1,0:T(8,128)S(1)} %bitcast_select_fusion.table_in), custom_call_target="tpu_custom_call" | custom-call | tf_op jit(solution)/shard_map/pallas_call | solution.py:343
  59.5 0.7 %copy.6 = f32[64,512]{1,0:T(8,128)} copy(f32[64,512]{1,0:T(8,128)S(1)} %shard_map.46) | data formatting | bytes 262144
Async XLA Ops:
  0.7 0.9 %copy-start = (f32[64,512]{1,0:T(8,128)S(1)}, f32[64,512]{1,0:T(8,128)}, u32[]{:S(2)}) copy-start(f32[64,512]{1,0:T(8,128)} %panel.1) | copy-start | bytes 393220

commit v6 on v5

--- a/solution.py
+++ b/solution.py
@@ -22,7 +22,7 @@
 Z_ORDER = (2, 1, 3)
 FAR, NEAR = pl.ds(0, 3), pl.ds(3, 1)
 NEAR_FAR = (1, 3, 2)
-PARTS = (1, 2)
+PARTS = (2, 2)
 
 
 def inverse_factor(gram):

time: 60.4 us -> 60.3 us (level)
  no operation moved by 1% of the time
where the time goes in v6:
time: 60.3 us; the launch traced here: 60.1 us
  Pallas kernels  57.9 us (96%)
  local copies, waits for them, and re-layouts  1.56 us (3%)
  other arithmetic  0.69 us (1%)
    pallas_call x1, Pallas kernels, per_device(): pl.pallas_call(kernel, out_shape=jax.ShapeDtypeStruct(panel.shape, F32),...  57.9 us
    unnamed x3, local copies, waits for them, and re-layouts  1.56 us

profile of v6, /device:TPU:1, one launch (start us, length us, event | category | flops | bytes accessed | tf_op | source)
XLA Modules:
  0.0 60.1 jit_solution(14709766797869532226)
XLA Ops:
  0.0 0.7 %bitcast_select_fusion.table_in = s32[8,16]{1,0:T(8,128)S(1)} fusion(s32[16,1,8]{0,2,1:T(8,128)} %param.6, s32[16]{0:T(128)} %bitcast.5), kind=kLoop, calls=%fused_computation | loop fusion | flops 256 | bytes 1088 | tf_op jit(solution)/shard_map/jit(_where)/select_n | solution.py:341
  0.7 0.0 copy-start
  0.7 0.9 %copy-done = f32[64,512]{1,0:T(8,128)S(1)} copy-done((f32[64,512]{1,0:T(8,128)S(1)}, f32[64,512]{1,0:T(8,128)}, u32[]{:S(2)}) %copy-start) | copy-done | bytes 131096
  1.6 57.9 %shard_map.46 = f32[64,512]{1,0:T(8,128)S(1)} custom-call(f32[64,512]{1,0:T(8,128)S(1)} %copy-done, bf16[16,1,8,256,256]{4,3,2,1,0:T(8,128)(2,1)} %blocks.1, s32[8,16]{1,0:T(8,128)S(1)} %bitcast_select_fusion.table_in), custom_call_target="tpu_custom_call" | custom-call | tf_op jit(solution)/shard_map/pallas_call | solution.py:343
  59.5 0.7 %copy.6 = f32[64,512]{1,0:T(8,128)} copy(f32[64,512]{1,0:T(8,128)S(1)} %shard_map.46) | data formatting | bytes 262144
Async XLA Ops:
  0.7 0.9 %copy-start = (f32[64,512]{1,0:T(8,128)S(1)}, f32[64,512]{1,0:T(8,128)}, u32[]{:S(2)}) copy-start(f32[64,512]{1,0:T(8,128)} %panel.1) | copy-start | bytes 393220
